TPU v7x, 256 devices: a whole 4x4x8 slice. The times are simulated.
256 devices in a mesh: ops: 8 (over z), sec: 32 (over y, x, core).
Axes of the slice: x: 4, y: 4, z: 8, core: 2. Of those that a mesh axis runs over, the one named last changes fastest.
Arguments:
- wavefunction: bfloat16 [2, 1024, 128, 128], P(None, 'sec'), may hold values from -6 to 6
- right_number: int32 [1024, 1], P('sec'), may hold values from 0 to 31; in each aligned block of 32 rows (0 to 31, 32 to 63, ...) at most 2 rows name the same one
- left_dim: int32 [32], P('sec'), may hold values from 64 to 128, as said below
- right_dim: int32 [32], P('sec'), may hold values from 64 to 128, as said below
- left_ops: bfloat16 [32, 32, 128, 128], P('ops', 'sec'), may hold values from -0.09375 to 0.09375
- right_ops: bfloat16 [32, 32, 128, 128], P('ops', 'sec'), may hold values from -0.5 to 0.5
- set_kind: int32 [32], P('ops'), may hold values from 0 to 1
Outputs:
- sigma: bfloat16 [2, 1024, 128, 128], P(None, 'sec')
- subspace: float32 [2, 2], replicated
Inputs may be any that keep to these rules, and one draw needn't show every extreme that they name: `right_number`: no more than 2 of the sectors s with the same s // 32 share a right quantum number; some such set has exactly 2. `left_dim`: some left quantum number has the full 128. `right_dim`: some right quantum number has the full 128.
All inputs are finite; a program needn't handle non-finite values.
Results may differ from a plain program's by a relative error of at most 0.005.
Values may be sent and summed in bfloat16 or wider, within the bound.
A program may use at most 128 MiB of HBM per device.

v0:
```python
import jax
import jax.numpy as jnp
from jax import lax
from jax.sharding import PartitionSpec as P


def body(wavefunction, right_number, left_dim, right_dim, left_ops, right_ops, set_kind):
    nvec = wavefunction.shape[0]
    sec_dev = wavefunction.shape[1]
    width = wavefunction.shape[-1]
    owners = lax.axis_size("sec")
    lanes = jnp.arange(width, dtype=jnp.int32)
    row_keep = lanes < left_dim[0]
    masked_block = jnp.where(
        row_keep[None, None, :, None], wavefunction, jnp.zeros_like(wavefunction)
    )
    slots_per = max(2, 2 * sec_dev // owners)
    target = right_number[:, 0]
    indicator_matrix = (target[:, None] == jnp.arange(owners, dtype=jnp.int32)[None, :]).astype(
        jnp.int32
    )
    before = jnp.cumsum(indicator_matrix, axis=0) - indicator_matrix
    rank_in = jnp.sum(before * indicator_matrix, axis=1)
    slot = target * slots_per + rank_in
    placer = (slot[:, None] == jnp.arange(owners * slots_per, dtype=jnp.int32)[None, :]).astype(
        jnp.bfloat16
    )
    outgoing = jnp.einsum(
        "st,vsab->tvab", placer, masked_block, preferred_element_type=jnp.float32
    ).astype(jnp.bfloat16)
    arrived = lax.all_to_all(outgoing, "sec", split_axis=0, concat_axis=0, tiled=True)
    column_retained = lanes < right_dim[0]
    arrived = jnp.where(column_retained[None, None, None, :], arrived, jnp.zeros_like(arrived))
    arrived = arrived.reshape(owners, slots_per * nvec, width, width)
    own_right = right_ops[:, 0]
    piece = lax.all_gather(left_ops, "sec", axis=1, tiled=True)
    turned = jnp.where(set_kind[:, None, None, None] == 1, jnp.swapaxes(piece, 2, 3), piece)
    inner_product = jnp.einsum(
        "jsab,kbc->jskac", arrived, own_right, preferred_element_type=jnp.float32
    ).astype(jnp.bfloat16)
    result = jnp.einsum(
        "kjea,jskac->jsec", turned, inner_product, preferred_element_type=jnp.float32
    )
    products = jnp.where(column_retained[None, None, None, :], result, 0.0)
    products = products.reshape(owners * slots_per, nvec, width, width)
    returned = lax.all_to_all(products, "sec", split_axis=0, concat_axis=0, tiled=True)
    partial_value = jnp.einsum(
        "st,tvab->vsab", placer.astype(jnp.float32), returned, precision=lax.Precision.HIGHEST
    )
    total = lax.psum(partial_value, "ops")
    sigma = jnp.where(row_keep[None, None, :, None], total, 0.0).astype(jnp.bfloat16)
    local_sum = jnp.einsum("vsab,wsab->vw", wavefunction, sigma, preferred_element_type=jnp.float32)
    scale = 1.0 / jnp.sqrt(jnp.float32(owners * sec_dev * width * width))
    subspace = lax.psum(local_sum, "sec") * scale
    return (sigma, subspace)


def solution(mesh):
    return jax.shard_map(
        body,
        mesh=mesh,
        in_specs=(
            P(None, "sec", None, None),
            P("sec", None),
            P("sec"),
            P("sec"),
            P("ops", "sec", None, None),
            P("ops", "sec", None, None),
            P("ops"),
        ),
        out_specs=(P(None, "sec", None, None), P()),
        check_vma=False,
    )
```

profile of v0, /device:TPU:1, one launch (start us, length us, event | category | flops | bytes accessed | tf_op | source)
XLA Modules:
  0.0 402.5 jit_solution(10988781554894586555)
XLA Ops:
  7.2 0.0 copy-start
  7.2 0.0 all-gather.2.cloned.1.call-start
  7.2 0.7 all-gather.2.cloned.1.call-update
  8.6 0.7 fusion.28
  9.3 0.1 reduce_window_sum.11
  9.3 0.8 select_reduce_fusion
  10.2 0.7 fusion.34
  10.9 3.6 convolution_convert_fusion
  14.5 4.7 %copy.27 = bf16[64,2,128,128]{3,2,1,0:T(8,128)(2,1)} copy(bf16[64,2,128,128]{3,0,2,1:T(8,128)(2,1)S(1)} %convolution_convert_fusion) | data formatting | bytes 8388608 | tf_op jit(solution)/shard_map/convert_element_type | solution.py:30
  19.1 0.0 copy-start.2
  19.2 8.8 %all-to-all-start = ((bf16[64,2,128,128]{3,2,1,0:T(8,128)(2,1)}), bf16[64,2,128,128]{3,2,1,0:T(8,128)(2,1)}, u32[]{:S(2)}, u32[]{:S(2)}) async-start(bf16[64,2,128,128]{3,2,1,0:T(8,128)(2,1)} %copy.27), calls=%async_computation | async-start | bytes 8388608 | tf_op jit(solution)/shard_map/all_to_all | solution.py:31
  28.6 0.0 copy-done.2
  28.6 54.1 %all-to-all-done = bf16[64,2,128,128]{3,2,1,0:T(8,128)(2,1)} async-done(((bf16[64,2,128,128]{3,2,1,0:T(8,128)(2,1)}), bf16[64,2,128,128]{3,2,1,0:T(8,128)(2,1)}, u32[]{:S(2)}, u32[]{:S(2)}) %all-to-all-start) | async-done | bytes 4194336 | tf_op jit(solution)/shard_map/all_to_all | solution.py:31
  82.7 4.4 %broadcast_select_fusion = bf16[64,2,128,128]{3,2,1,0:T(8,128)(2,1)} fusion(bf16[64,2,128,128]{3,2,1,0:T(8,128)(2,1)} %all-to-all-done, pred[128]{0:T(512)(128)(4,1)S(1)} %iota_compare_fusion.2), kind=kLoop, calls=%fused_computation.11 | loop fusion | flops 2097152 | bytes 8388736 | tf_op jit(solution)/shard_map/jit(_where)/select_n | solution.py:33
  87.1 4.1 %all-gather.2.cloned.1.call-done = bf16[4,32,128,128]{3,2,1,0:T(8,128)(2,1)} async-done(((bf16[4,1,128,128]{3,2,1,0:T(8,128)(2,1)}), bf16[4,32,128,128]{3,2,1,0:T(8,128)(2,1)}) %all-gather.2.cloned.1.call-update) | async-done | bytes 4194320 | tf_op jit(solution)/shard_map/all_gather | solution.py:36
  91.2 6.4 %copy.28 = bf16[4,32,128,128]{2,3,1,0:T(8,128)(2,1)} copy(bf16[4,32,128,128]{3,2,1,0:T(8,128)(2,1)} %all-gather.2.cloned.1.call-done) | data formatting | bytes 8388608 | tf_op jit(solution)/shard_map/all_gather | solution.py:36
  97.6 0.0 copy-done
  97.6 14.0 %bitcast_select_fusion = f32[32,4,128,128]{3,2,1,0:T(8,128)} fusion(pred[128]{0:T(512)(128)(4,1)S(1)} %iota_compare_fusion.2, bf16[32,4,128,128,1]{3,2,4,1,0:T(8,128)(2,1)} %bitcast.61, bf16[4,1,128,128]{3,2,1,0:T(8,128)(2,1)S(1)} %copy-done, bf16[4,32,128,128]{3,2,1,0:T(8,128)(2,1)} %all-gather.2.cloned.1.call-done, bf16[4,32,128,128]{2,3,1,0:T(8,128)(2,1)} %copy.28, ...), kind=kOutput, calls=%fused_computation.4 | convolution fusion | flops 4307550208 | bytes 21102724 | tf_op jit(solution)/shard_map/kjea,jskac->jsec/dot_general | solution.py:41
  111.6 9.0 %copy.31 = f32[64,2,128,128]{3,2,1,0:T(8,128)} copy(f32[64,2,128,128]{2,3,1,0:T(8,128)} %bitcast.60) | data formatting | bytes 16777216 | tf_op jit(solution)/shard_map/reshape | solution.py:45
  120.6 101.1 %all_to_all.10 = f32[64,2,128,128]{3,2,1,0:T(8,128)S(1)} all-to-all(f32[64,2,128,128]{3,2,1,0:T(8,128)} %copy.31), channel_id=1, replica_groups=mesh['ops'=8,'sec'=32] {'sec'}, dimensions={0} | all-to-all | bytes 16777216 | tf_op jit(solution)/shard_map/all_to_all | solution.py:46
  221.7 7.7 %fusion.9 = f32[2,32,128,128]{3,1,2,0:T(8,128)} fusion(f32[64,2,128,128]{3,2,1,0:T(8,128)S(1)} %all_to_all.10, s32[32]{0:T(128)S(1)} %fusion.34), kind=kOutput, calls=%fused_computation.13 | convolution fusion | flops 805308416 | bytes 12583040 | tf_op jit(solution)/shard_map/st,tvab->vsab/dot_general | solution.py:47
  229.4 90.7 %all-reduce.1 = bf16[2,32,128,128]{3,1,2,0:T(8,128)(2,1)S(1)} all-reduce(f32[2,32,128,128]{3,1,2,0:T(8,128)} %fusion.9), channel_id=1, replica_groups=mesh['ops'=8,'sec'=32] {'ops'}, use_global_device_ids=true, to_apply=%region_2.3 | all-reduce | flops 1048576 | bytes 6291456 | tf_op jit(solution)/shard_map/psum | solution.py:50
  320.1 0.0 copy-start.1
  320.1 0.5 select_convert_fusion
  320.6 1.1 copy-done.1
  321.7 7.2 %fusion.20 = f32[2,2]{0,1:T(2,128)S(1)} fusion(bf16[2,32,128,128]{3,2,1,0:T(8,128)(2,1)S(1)} %copy-done.1, bf16[2,32,128,128]{3,1,2,0:T(8,128)(2,1)S(1)} %select_convert_fusion), kind=kOutput, calls=%fused_computation.19 | convolution fusion | flops 4194304 | bytes 4194320 | tf_op jit(solution)/shard_map/vsab,wsab->vw/dot_general | solution.py:52
  328.9 2.2 copy.35
  331.1 63.9 %psum.15 = f32[2,2]{0,1:T(2,128)S(1)} all-reduce(f32[2,2]{0,1:T(2,128)S(1)} %fusion.20), channel_id=1, replica_groups=mesh['ops'=8,'sec'=32] {'sec'}, use_global_device_ids=true, to_apply=%region_3.4 | all-reduce | flops 4 | bytes 32 | tf_op jit(solution)/shard_map/psum | solution.py:54
  395.0 0.7 copy.36
  (4 shorter events, 0.0 us)
Async XLA Ops:
  7.2 90.4 %copy-start = (bf16[4,1,128,128]{3,2,1,0:T(8,128)(2,1)S(1)}, bf16[4,1,128,128]{3,2,1,0:T(8,128)(2,1)}, u32[]{:S(2)}) copy-start(bf16[4,1,128,128]{3,2,1,0:T(8,128)(2,1)} %param.12) | copy-start | bytes 393220
  7.2 84.0 %all-gather.2.cloned.1.call-start = ((), (), s32[]{:S(2)}) async-start(), calls=%async_computation.2 | async-start | bytes 4325376 | tf_op jit(solution)/shard_map/all_gather | solution.py:36
  19.1 9.5 %copy-start.2 = (s32[4]{0:T(128)S(1)}, s32[4]{0:T(128)}, u32[]{:S(2)}) copy-start(s32[4]{0:T(128)} %param.13) | copy-start | bytes 52
  19.2 63.6 %all-to-all-start = ((bf16[64,2,128,128]{3,2,1,0:T(8,128)(2,1)}), bf16[64,2,128,128]{3,2,1,0:T(8,128)(2,1)}, u32[]{:S(2)}, u32[]{:S(2)}) async-start(bf16[64,2,128,128]{3,2,1,0:T(8,128)(2,1)} %copy.27), calls=%async_computation | async-start | bytes 8388608 | tf_op jit(solution)/shard_map/all_to_all | solution.py:31
  320.1 1.6 copy-start.1
Sparse Core Ops, SparseCore 0:
  10.6 80.5 all-gather.1
where the time goes:
time: 403 us; the launch traced here: 402 us
  blocking collectives  256 us (64%)
  waiting for transfers between devices  58.8 us (15%)
  matrix products  32.6 us (8%)
  local copies, waits for them, and re-layouts  24 us (6%)
  between operations  15.4 us (4%)
  starting transfers between devices  8.82 us (2%)
  other arithmetic  7.23 us (2%)
    all_to_all x1, blocking collectives, body(): lax.all_to_all(products, 'sec', split_axis=0, concat_axis=0, tiled=True)  101 us
    psum x1, blocking collectives, body(): total = lax.psum(partial_value, 'ops')  90.7 us
    psum x1, blocking collectives, body(): subspace = lax.psum(local_sum, 'sec') * scale  63.9 us
    all_to_all x1, waiting for transfers between devices, body(): lax.all_to_all(outgoing, 'sec', split_axis=0, concat_axis=0, tiled=True)  54.1 us
    dot_general x1, matrix products, body(): jnp.einsum('kjea,jskac->jsec', turned, inner_product, preferred_element_t...  14 us
    reshape x1, local copies, waits for them, and re-layouts, body(): products = products.reshape(owners * slots_per, nvec, width, width)  9.01 us
    all_to_all x1, starting transfers between devices, body(): lax.all_to_all(outgoing, 'sec', split_axis=0, concat_axis=0, tiled=True)  8.78 us
  transfers between devices with their start and end apart: 2, of which 2 were waited for; matrix products, arithmetic and copies ran while one was open for 4% of the time, Pallas kernels for 0%

commit v1 on v0

v1 whole, which is shorter than its diff:
```python
import functools
import math

import jax
import jax.numpy as jnp
from jax import lax
from jax.experimental import pallas as pl
from jax.experimental.pallas import tpu as pltpu
from jax.sharding import PartitionSpec as P

MESH = pl.DeviceIdType.MESH
BF16 = jnp.bfloat16
F32 = jnp.float32


def remote(src, dst, send, recv, device):
    return pltpu.make_async_remote_copy(
        src_ref=src, dst_ref=dst, send_sem=send, recv_sem=recv, device_id=device, device_id_type=MESH
    )


class Ring:
    def __init__(self, n, me, device, slot, half, send, recv):
        self.n, self.me, self.device = n, me, device
        self.slot, self.half, self.send, self.recv = slot, half, send, recv
        self.sent = []

    def at(self, offset):
        return lax.rem(self.me + (offset + self.n), self.n)

    def ref(self, offset, distance, way):
        if 2 * distance == self.n:
            return self.half(self.at(offset), way)
        return self.slot(self.at(offset))

    def pass_on(self, distance, way):
        step = 1 if way == 0 else -1
        block = self.ref(-step * (distance - 1), distance, way)
        index = way * (self.n // 2) + distance - 1
        copy = remote(block, block, self.send(index), self.recv(index), self.device(self.at(step)))
        copy.start()
        self.sent.append(copy)

    def start(self):
        if self.n > 1:
            self.pass_on(1, 0)
            self.pass_on(1, 1)

    def step(self, distance):
        if 2 * distance > self.n:
            return
        for way in range(2):
            step = 1 if way == 0 else -1
            block = self.ref(-step * distance, distance, way)
            index = way * (self.n // 2) + distance - 1
            remote(block, block, self.send(index), self.recv(index), self.device(self.at(step))).wait_recv()
            if 2 * (distance + 1) <= self.n:
                self.pass_on(distance + 1, way)

    def finish(self):
        for copy in self.sent:
            copy.wait_send()
        self.sent = []


def kernel(
    planes, side, chunk,
    w_hbm, number, left_dim, right_dim, left_ops, right_ops, kind,
    out, sub,
    w, rt, rg, lg, inner, sg, turned, red,
    w_sem, a2a_send, a2a_recv, ring_send, ring_recv, sib_send, sib_recv, red_send, red_recv,
):
    terms, width = left_ops.shape[0], left_ops.shape[-1]
    nvec, sectors = w.shape[0], w.shape[1]
    part = width // planes
    chunks = sectors // chunk
    rows = nvec * part
    plane = lax.axis_index("ops")
    place = lax.axis_index("sec")
    core = lax.rem(place, 2)
    chip = place // 2
    px, py = lax.rem(chip, side), chip // side
    first = px * (1 - core) + py * core
    second = py * (1 - core) + px * core

    def sector_of(one, two, c):
        x = one * (1 - c) + two * c
        y = two * (1 - c) + one * c
        return 2 * (y * side + x) + c

    def shift(base, offset, n):
        return lax.rem(base + (offset + n), n)

    above = [{"ops": shift(plane, d, planes)} for d in range(1, planes)]
    along = [{"sec": sector_of(shift(first, d, side), second, core)} for d in range(1, side)]
    across = [{"sec": sector_of(first, shift(second, d, side), core)} for d in range(1, side)]
    sibling = {"sec": place + 1 - 2 * core}

    barrier = pltpu.get_barrier_semaphore()
    partners = above + along + across + [sibling]
    for device in partners:
        pl.semaphore_signal(barrier, inc=1, device_id=device, device_id_type=MESH)

    w_copy = pltpu.make_async_copy(w_hbm, w, w_sem)
    w_copy.start()

    lane = lax.broadcasted_iota(jnp.int32, (width, width), 1)
    sub_lane = lax.broadcasted_iota(jnp.int32, (width, width), 0)
    right_keep = (lane < right_dim[0]) & (sub_lane < right_dim[0])
    left_keep = (lane < left_dim[0]) & (sub_lane < left_dim[0])
    for k in range(terms):
        block = jnp.where(right_keep, right_ops[k, 0].astype(F32), 0.0).T.astype(BF16)
        for o in range(planes):
            rt[o, k * part:(k + 1) * part] = block[o * part:(o + 1) * part]
    for k in range(terms):
        block = jnp.where(left_keep, left_ops[k, 0].astype(F32), 0.0)
        normal = (jnp.zeros((width, width), jnp.int32) + kind[k]) == 0
        lg[plane, k * width:(k + 1) * width] = jnp.where(normal, block.T, block).astype(BF16)
    rg[place, pl.ds(pl.multiple_of(plane * (terms * part), terms * part), terms * part)] = rt[plane]

    pl.semaphore_wait(barrier, len(partners))

    def a2a(d):
        to = shift(plane, d, planes)
        piece = rg.at[place, pl.ds(pl.multiple_of(plane * (terms * part), terms * part), terms * part)]
        return remote(rt.at[to], piece, a2a_send.at[d - 1], a2a_recv.at[d - 1], {"ops": to})

    def a2a_arrival(d):
        source = shift(plane, -d, planes)
        piece = rg.at[place, pl.ds(pl.multiple_of(source * (terms * part), terms * part), terms * part)]
        return remote(piece, piece, a2a_send.at[d - 1], a2a_recv.at[d - 1], {"ops": shift(plane, d, planes)})

    slices = [a2a(d) for d in range(1, planes)]
    for copy in slices:
        copy.start()

    count = [0]

    def ring(n, me, device, slot, half):
        index = count[0]
        count[0] += 1
        return Ring(n, me, device, slot, half, lambda i: ring_send.at[index, i], lambda i: ring_recv.at[index, i])

    big = rg.shape[1]

    def half_rows(h, total):
        return pl.ds(h * (total // 2), total // 2)

    left = ring(
        planes, plane, lambda q: {"ops": q}, lambda q: lg.at[q], lambda q, h: lg.at[q, half_rows(h, lg.shape[1])]
    )
    one = ring(
        side, first, lambda q: {"sec": sector_of(q, second, core)},
        lambda q: rg.at[sector_of(q, second, core)],
        lambda q, h: rg.at[sector_of(q, second, core), half_rows(h, big)],
    )

    def second_ring(offset):
        line = shift(first, offset, side)
        return ring(
            side, second, lambda q: {"sec": sector_of(first, q, core)},
            lambda q: rg.at[sector_of(line, q, core)],
            lambda q, h: rg.at[sector_of(line, q, core), half_rows(h, big)],
        )

    two = [second_ring(offset) for offset in range(side)]
    handed = []

    def hand(d1, d2):
        block = rg.at[sector_of(shift(first, d1, side), shift(second, d2, side), core)]
        index = d1 * side + d2
        copy = remote(block, block, sib_send.at[index], sib_recv.at[index], sibling)
        copy.start()
        handed.append(copy)

    def handed_over(d1, d2):
        block = rg.at[sector_of(shift(second, d1, side), shift(first, d2, side), 1 - core)]
        index = d1 * side + d2
        remote(block, block, sib_send.at[index], sib_recv.at[index], sibling).wait_recv()

    left.start()
    for d in range(1, planes):
        a2a_arrival(d).wait_recv()
    one.start()
    two[0].start()
    hand(0, 0)
    if side == 4:
        one.step(1)
        two[1].start()
        two[3].start()
        hand(1, 0)
        hand(3, 0)
        two[0].step(1)
        hand(0, 1)
        hand(0, 3)
        left.step(1)
        one.step(2)
        two[2].start()
        hand(2, 0)
        for j in (1, 3):
            two[j].step(1)
            hand(j, 1)
            hand(j, 3)
        left.step(2)
        two[0].step(2)
        hand(0, 2)
        two[2].step(1)
        hand(2, 1)
        hand(2, 3)
        left.step(3)
        for j in (1, 3, 2):
            two[j].step(2)
            hand(j, 2)
    else:
        for d in (1, 2, 3):
            left.step(d)
    left.step(4)
    for d1 in range(side):
        for d2 in range(side):
            handed_over(d1, d2)
    w_copy.wait()

    chunk_rows = chunk * rows

    def sigma_ring(j):
        return ring(
            planes, plane, lambda q: {"ops": q}, lambda q: sg.at[j, q],
            lambda q, h: sg.at[j, q, half_rows(h, chunk_rows)],
        )

    sigma_rings = [sigma_ring(j) for j in range(chunks)]
    all_terms = terms * planes

    def compute(j):
        for i in range(chunk):
            s = j * chunk + i
            right = rg[number[s, 0]]
            block = w[:, s].reshape(nvec * width, width)
            product = lax.dot_general(
                right, block, (((1,), (1,)), ((), ())), preferred_element_type=F32
            ).astype(BF16)
            for k in range(all_terms):
                for v in range(nvec):
                    inner[i * rows + v * part:i * rows + (v + 1) * part, k * width:(k + 1) * width] = product[
                        k * part:(k + 1) * part, v * width:(v + 1) * width
                    ]
        total = jnp.dot(
            inner[...], lg[...].reshape(all_terms * width, width), preferred_element_type=F32
        ).astype(BF16)
        sg[j, plane] = total
        for i in range(chunk):
            s = j * chunk + i
            turned[:, s * width:(s + 1) * width] = total[i * rows:(i + 1) * rows]

    def assemble(j):
        for i in range(chunk):
            for v in range(nvec):
                low = i * rows + v * part
                block = sg[j, :, low:low + part].reshape(width, width)
                out[v, j * chunk + i] = block.T

    reductions = []

    def reduce_sends(stage, mine, n, devices):
        for d in range(1, n):
            copy = remote(
                red.at[stage, mine], red.at[stage, mine], red_send.at[stage, d - 1], red_recv.at[stage, d - 1],
                devices[d - 1],
            )
            copy.start()
            reductions.append(copy)

    def reduce_sum(stage, mine, n, devices):
        for d in range(1, n):
            slot = red.at[stage, shift(mine, -d, n)]
            remote(slot, slot, red_send.at[stage, d - 1], red_recv.at[stage, d - 1], devices[d - 1]).wait_recv()
        total = red[stage, 0]
        for i in range(1, n):
            total = total + red[stage, i]
        return total

    stages = [(plane, planes, above), (first, side, along), (second, side, across), (core, 2, [sibling])]

    def subspace_start():
        row = lax.broadcasted_iota(jnp.int32, (rows, width), 0)
        column = lax.broadcasted_iota(jnp.int32, (rows, width), 1)
        own = column == lax.rem(row, part) + plane * part
        tile_row = lax.broadcasted_iota(jnp.int32, red.shape[-2:], 0)
        tile_column = lax.broadcasted_iota(jnp.int32, red.shape[-2:], 1)
        tile = jnp.zeros(red.shape[-2:], F32)
        for i in range(nvec):
            product = jnp.dot(
                turned[...], w[i].reshape(sectors * width, width), preferred_element_type=F32
            )
            product = jnp.where(own, product, 0.0)
            for j in range(nvec):
                value = jnp.sum(product[j * part:(j + 1) * part], axis=(0, 1), keepdims=True)
                tile = tile + jnp.where((tile_row == i) & (tile_column == j), value, 0.0)
        red[0, plane] = tile
        reduce_sends(0, *stages[0])

    def subspace_stage(stage):
        total = reduce_sum(stage, *stages[stage])
        if stage + 1 < len(stages):
            red[stage + 1, stages[stage + 1][0]] = total
            reduce_sends(stage + 1, *stages[stage + 1])
        else:
            sub[...] = total * (1.0 / math.sqrt(2 * side * side * sectors * width * width))

    far = planes // 2
    for t in range(chunks + max(far, 4)):
        if t < chunks:
            compute(t)
            sigma_rings[t].start()
        for j in range(chunks):
            d = t - j
            if 1 <= d <= far:
                sigma_rings[j].step(d)
                if d == far:
                    assemble(j)
            elif planes == 1 and d == 1:
                assemble(j)
        if t == chunks - 1:
            subspace_start()
        elif t >= chunks and t - chunks < len(stages):
            subspace_stage(t - chunks)

    for copy in slices + handed + reductions:
        copy.wait_send()
    for each in [left, one] + two + sigma_rings:
        each.finish()


def body(wavefunction, right_number, left_dim, right_dim, left_ops, right_ops, set_kind, *, chunk=4):
    nvec, sectors, width, _ = wavefunction.shape
    planes = lax.axis_size("ops")
    places = lax.axis_size("sec")
    side = math.isqrt(places // 2)
    terms = left_ops.shape[0]
    part = width // planes
    rows = nvec * part
    chunks = sectors // chunk
    rings = 2 + side + chunks
    vmem = pl.BlockSpec(memory_space=pltpu.VMEM)
    smem = pl.BlockSpec(memory_space=pltpu.SMEM)
    dma = pltpu.SemaphoreType.DMA
    most = max(planes - 1, side - 1, 1)
    out, sub = pl.pallas_call(
        functools.partial(kernel, planes, side, chunk),
        out_shape=(
            jax.ShapeDtypeStruct(wavefunction.shape, BF16),
            jax.ShapeDtypeStruct((8, 128), F32),
        ),
        in_specs=[pl.BlockSpec(memory_space=pl.ANY), smem, smem, smem, vmem, vmem, smem],
        out_specs=(vmem, vmem),
        scratch_shapes=[
            pltpu.VMEM(wavefunction.shape, BF16),
            pltpu.VMEM((planes, terms * part, width), BF16),
            pltpu.VMEM((places, planes * terms * part, width), BF16),
            pltpu.VMEM((planes, terms * width, width), BF16),
            pltpu.VMEM((chunk * rows, planes * terms * width), BF16),
            pltpu.VMEM((chunks, planes, chunk * rows, width), BF16),
            pltpu.VMEM((rows, sectors * width), BF16),
            pltpu.VMEM((4, max(planes, side, 2), 8, 128), F32),
            dma(()),
            dma((max(planes - 1, 1),)),
            dma((max(planes - 1, 1),)),
            dma((rings, max(planes, side))),
            dma((rings, max(planes, side))),
            dma((side * side,)),
            dma((side * side,)),
            dma((4, most)),
            dma((4, most)),
        ],
        compiler_params=pltpu.CompilerParams(
            collective_id=0, has_side_effects=True, vmem_limit_bytes=48 * 1024 * 1024
        ),
        cost_estimate=pl.CostEstimate(
            flops=4 * sectors * nvec * terms * width**3, bytes_accessed=6 * 1024 * 1024, transcendentals=0
        ),
    )(wavefunction, right_number, left_dim, right_dim, left_ops, right_ops, set_kind)
    return out, sub[:nvec, :nvec]


def solution(mesh):
    return jax.shard_map(
        body,
        mesh=mesh,
        in_specs=(
            P(None, "sec", None, None),
            P("sec", None),
            P("sec"),
            P("sec"),
            P("ops", "sec", None, None),
            P("ops", "sec", None, None),
            P("ops"),
        ),
        out_specs=(P(None, "sec", None, None), P()),
        check_vma=False,
    )
```

time: 403 us -> 90.7 us (0.23)
  blocking collectives: 256 us -> 0 us
  Pallas kernels: 0 us -> 81.9 us
  waiting for transfers between devices: 58.8 us -> 0 us
  matrix products: 32.6 us -> 0 us
  local copies, waits for them, and re-layouts: 24 us -> 6.67 us
  between operations: 15.4 us -> 1.94 us
  starting transfers between devices: 8.82 us -> 0 us
  other arithmetic: 7.23 us -> 0 us
    psum x2 -> x0, blocking collectives: 155 us -> none  [the longest x1 90.7 us: body(): total = lax.psum(partial_value, 'ops')]
    all_to_all x1 -> x0, blocking collectives: 101 us -> none  [body(): lax.all_to_all(products, 'sec', split_axis=0, concat_axis=0, tiled=True)]
    pallas_call x0 -> x1, Pallas kernels: none -> 81.9 us  [body(): pl.pallas_call(functools.partial(kernel, planes, side, chunk), out_shape=...]
    all_to_all x1 -> x0, waiting for transfers between devices: 54.1 us -> none  [body(): lax.all_to_all(outgoing, 'sec', split_axis=0, concat_axis=0, tiled=True)]
    dot_general x4 -> x0, matrix products: 32.6 us -> none  [the longest x1 14 us: body(): jnp.einsum('kjea,jskac->jsec', turned, inner_product, preferred_element_t...]
    reshape x1 -> x0, local copies, waits for them, and re-layouts: 9.01 us -> none  [body(): products = products.reshape(owners * slots_per, nvec, width, width)]
    all_to_all x1 -> x0, starting transfers between devices: 8.78 us -> none  [body(): lax.all_to_all(outgoing, 'sec', split_axis=0, concat_axis=0, tiled=True)]
    all_gather x1 -> x0, local copies, waits for them, and re-layouts: 6.37 us -> none  [body(): piece = lax.all_gather(left_ops, 'sec', axis=1, tiled=True)]
  transfers between devices with their start and end apart: 2 -> 0, of which waited for: 2 -> 0; matrix products, arithmetic and copies ran while one was open for 4% -> 0% of each run, Pallas kernels for 0% -> 0%
where the time goes in v1:
time: 90.7 us; the launch traced here: 90.5 us
  Pallas kernels  81.9 us (90%)
  local copies, waits for them, and re-layouts  6.67 us (7%)
  between operations  1.94 us (2%)
    pallas_call x1, Pallas kernels, body(): pl.pallas_call(functools.partial(kernel, planes, side, chunk), out_shape=...  81.9 us
    unnamed x10, local copies, waits for them, and re-layouts  6.11 us

profile of v1, /device:TPU:1, one launch (start us, length us, event | category | flops | bytes accessed | tf_op | source)
XLA Modules:
  0.0 90.5 jit_solution(17421028515920250013)
XLA Ops:
  1.9 0.7 copy.9.number
  2.7 0.0 copy-start
  2.7 1.6 %copy-done = bf16[2,32,128,128]{3,2,1,0:T(8,128)(2,1)S(1)} copy-done((bf16[2,32,128,128]{3,2,1,0:T(8,128)(2,1)S(1)}, bf16[2,32,128,128]{3,2,1,0:T(8,128)(2,1)}, u32[]{:S(2)}) %copy-start) | copy-done | bytes 2097176
  4.3 0.0 copy-start.1
  4.3 0.9 copy-done.1
  5.2 0.0 copy-start.2
  5.2 0.9 copy-done.2
  6.1 0.0 copy-start.3
  6.1 0.7 copy-done.3
  6.7 81.9 %shard_map.86 = (bf16[2,32,128,128]{3,2,1,0:T(8,128)(2,1)S(1)}, f32[8,128]{1,0:T(8,128)S(1)}) custom-call(bf16[2,32,128,128]{3,2,1,0:T(8,128)(2,1)S(1)} %copy-done, s32[32,1]{1,0:T(8,128)S(1)} %copy.9.number, s32[1]{0:T(128)S(6)} %copy.11.left_dim, s32[1]{0:T(128)S(6)} %copy.12.right_dim, bf16[4,1,128,128]{3,2,1,0:T(8,128)(2,1)S(1)} %copy-done.1, ...), custom_call_target="tpu_custom_call" | custom-call | flops 2147483648 | bytes 6291456 | tf_op jit(solution)/shard_map/pallas_call | solution.py:348
  88.7 0.6 slice.3
  89.2 1.3 %copy.13 = bf16[2,32,128,128]{3,2,1,0:T(8,128)(2,1)} copy(bf16[2,32,128,128]{3,2,1,0:T(8,128)(2,1)S(1)} %get-tuple-element.8) | data formatting | bytes 4194304
Async XLA Ops:
  2.7 1.6 %copy-start = (bf16[2,32,128,128]{3,2,1,0:T(8,128)(2,1)S(1)}, bf16[2,32,128,128]{3,2,1,0:T(8,128)(2,1)}, u32[]{:S(2)}) copy-start(bf16[2,32,128,128]{3,2,1,0:T(8,128)(2,1)} %w_hbm.1) | copy-start | bytes 6291460
  4.3 0.9 copy-start.1
  5.2 0.9 copy-start.2
  6.1 0.7 copy-start.3

commit v2 on v1

v2 whole, which is shorter than its diff:
```python
import functools
import math

import jax
import jax.numpy as jnp
from jax import lax
from jax.experimental import pallas as pl
from jax.experimental.pallas import tpu as pltpu
from jax.sharding import PartitionSpec as P

MESH = pl.DeviceIdType.MESH
BF16 = jnp.bfloat16
F32 = jnp.float32


def remote(src, dst, send, recv, device):
    return pltpu.make_async_remote_copy(
        src_ref=src, dst_ref=dst, send_sem=send, recv_sem=recv, device_id=device, device_id_type=MESH
    )


class Ring:
    def __init__(self, n, me, device, slot, half, send, recv):
        self.n, self.me, self.device = n, me, device
        self.slot, self.half, self.send, self.recv = slot, half, send, recv
        self.sent = []

    def at(self, offset):
        return lax.rem(self.me + (offset + self.n), self.n)

    def ref(self, offset, distance, way):
        if 2 * distance == self.n:
            return self.half(self.at(offset), way)
        return self.slot(self.at(offset))

    def pass_on(self, distance, way):
        step = 1 if way == 0 else -1
        block = self.ref(-step * (distance - 1), distance, way)
        index = way * (self.n // 2) + distance - 1
        copy = remote(block, block, self.send(index), self.recv(index), self.device(self.at(step)))
        copy.start()
        self.sent.append(copy)

    def start(self):
        if self.n > 1:
            self.pass_on(1, 0)
            self.pass_on(1, 1)

    def step(self, distance):
        if 2 * distance > self.n:
            return
        for way in range(2):
            step = 1 if way == 0 else -1
            block = self.ref(-step * distance, distance, way)
            index = way * (self.n // 2) + distance - 1
            remote(block, block, self.send(index), self.recv(index), self.device(self.at(step))).wait_recv()
            if 2 * (distance + 1) <= self.n:
                self.pass_on(distance + 1, way)

    def finish(self):
        for copy in self.sent:
            copy.wait_send()
        self.sent = []


def kernel(
    planes, side, chunk,
    w_hbm, number_hbm, left_dim_hbm, right_dim_hbm, left_hbm, right_hbm, kind_hbm,
    out, sub,
    w, number, left_dim, right_dim, left_ops, right_ops, kind, rt, rg_low, rg_high, lg, inner, sg, turned, red,
    in_sem, a2a_send, a2a_recv, first_send, first_recv, second_send, second_recv,
    ring_send, ring_recv, sib_send, sib_recv, red_send, red_recv,
):
    terms, width = left_ops.shape[0], left_ops.shape[-1]
    nvec, sectors = w.shape[0], w.shape[1]
    part = width // planes // 2
    rows = nvec * part
    span = terms * part
    chunks = sectors // chunk
    all_terms = terms * planes
    plane = lax.axis_index("ops")
    place = lax.axis_index("sec")
    core = lax.rem(place, 2)
    chip = place // 2
    px, py = lax.rem(chip, side), chip // side
    first = px * (1 - core) + py * core
    second = py * (1 - core) + px * core

    def sector_of(one, two, c):
        x = one * (1 - c) + two * c
        y = two * (1 - c) + one * c
        return 2 * (y * side + x) + c

    def shift(base, offset, n):
        return lax.rem(base + (offset + n), n)

    above = [{"ops": shift(plane, d, planes)} for d in range(1, planes)]
    along = [{"sec": sector_of(shift(first, d, side), second, core)} for d in range(1, side)]
    across = [{"sec": sector_of(first, shift(second, d, side), core)} for d in range(1, side)]
    sibling = {"sec": place + 1 - 2 * core}

    barrier = pltpu.get_barrier_semaphore()
    partners = above + along + across + [sibling]
    for device in partners:
        pl.semaphore_signal(barrier, inc=1, device_id=device, device_id_type=MESH)

    loads = [
        pltpu.make_async_copy(a, b, in_sem.at[i])
        for i, (a, b) in enumerate([
            (right_hbm, right_ops), (right_dim_hbm, right_dim), (left_hbm, left_ops), (left_dim_hbm, left_dim),
            (kind_hbm, kind), (number_hbm, number), (w_hbm, w),
        ])
    ]
    for copy in loads:
        copy.start()

    rg = (rg_low, rg_high)
    lane = lax.broadcasted_iota(jnp.int32, (width, width), 1)
    sub_lane = lax.broadcasted_iota(jnp.int32, (width, width), 0)
    loads[0].wait()
    loads[1].wait()
    right_keep = (lane < right_dim[0]) & (sub_lane < right_dim[0])
    blocks = [jnp.where(right_keep, right_ops[k, 0].astype(F32), 0.0).T for k in range(terms)]
    for o in range(planes):
        for h in range(2):
            low = (h * planes + o) * part
            rt[o, h] = jnp.concatenate([block[low:low + part] for block in blocks], axis=0).astype(BF16)

    def slot(r, h, o):
        return rg[h].at[r, pl.ds(pl.multiple_of(o * span, span), span)]

    for h in range(2):
        rg[h][place, pl.ds(pl.multiple_of(plane * span, span), span)] = rt[plane, h]
    for copy in loads[2:5]:
        copy.wait()
    left_keep = (lane < left_dim[0]) & (sub_lane < left_dim[0])
    for k in range(terms):
        block = jnp.where(left_keep, left_ops[k, 0].astype(F32), 0.0)
        normal = (jnp.zeros((width, width), jnp.int32) + kind[k]) == 0
        lg[plane, k * width:(k + 1) * width] = jnp.where(normal, block.T, block).astype(BF16)

    pl.semaphore_wait(barrier, len(partners))
    sends = []

    def send(src, dst, send_sem, recv_sem, device):
        copy = remote(src, dst, send_sem, recv_sem, device)
        copy.start()
        sends.append(copy)

    def arrived(ref, send_sem, recv_sem):
        remote(ref, ref, send_sem, recv_sem, sibling).wait_recv()

    far_first = sorted(range(1, planes), key=lambda d: -min(d, planes - d))
    for h in range(2):
        for d in far_first:
            to = shift(plane, d, planes)
            send(rt.at[to, h], slot(place, h, plane), a2a_send.at[h, d], a2a_recv.at[h, d], {"ops": to})

    rings = [0]

    def ring(slot_of, half_of):
        index = rings[0]
        rings[0] += 1
        return Ring(
            planes, plane, lambda q: {"ops": q}, slot_of, half_of,
            lambda i: ring_send.at[index, i], lambda i: ring_recv.at[index, i],
        )

    pieces = 2
    deep = terms * width // pieces

    def left_ring(i):
        return ring(
            lambda q: lg.at[q, pl.ds(i * deep, deep)],
            lambda q, h: lg.at[q, pl.ds(i * deep + h * (deep // 2), deep // 2)],
        )

    left = [left_ring(i) for i in range(pieces)]

    def left_step(d):
        for each in left:
            each.step(d)

    for each in left:
        each.start()

    order = [d for d in (1, 3, 2) if d < side]

    def block(h, j, d):
        return rg[h].at[sector_of(shift(first, -j, side), shift(second, -d, side), core)]

    def first_sends(h):
        for d in reversed(order):
            send(block(h, 0, 0), block(h, 0, 0), first_send.at[h, d], first_recv.at[h, d], along[d - 1])

    def first_arrival(h, d):
        arrived(block(h, d, 0), first_send.at[h, d], first_recv.at[h, d])

    def second_sends(h, j):
        for d in order:
            send(block(h, j, 0), block(h, j, 0), second_send.at[h, j, d], second_recv.at[h, j, d], across[d - 1])

    def second_arrival(h, j, d):
        arrived(block(h, j, d), second_send.at[h, j, d], second_recv.at[h, j, d])

    def hand(h, j, d):
        send(block(h, j, d), block(h, j, d), sib_send.at[h, j, d], sib_recv.at[h, j, d], sibling)

    def handed(h):
        for j in range(side):
            for d in range(side):
                theirs = rg[h].at[sector_of(shift(second, -j, side), shift(first, -d, side), 1 - core)]
                arrived(theirs, sib_send.at[h, j, d], sib_recv.at[h, j, d])

    for h in range(2):
        for d in reversed(far_first):
            arrived(slot(place, h, shift(plane, -d, planes)), a2a_send.at[h, d], a2a_recv.at[h, d])
        first_sends(h)
        second_sends(h, 0)
        hand(h, 0, 0)
    left_step(1)
    for h in range(2):
        for j in order:
            first_arrival(h, j)
            second_sends(h, j)
            hand(h, j, 0)
        if h == 0:
            left_step(2)

    def second_arrivals(h):
        for j in [0] + order:
            for d in order:
                second_arrival(h, j, d)
                hand(h, j, d)
            if h == 0 and j == 0:
                left_step(3)

    second_arrivals(0)
    left_step(4)
    for copy in loads[5:]:
        copy.wait()
    handed(0)

    def sigma_ring(h, j):
        half = chunk * rows // 2
        return ring(
            lambda q: sg.at[h, j, q], lambda q, way: sg.at[h, j, q, pl.ds(way * half, half)]
        )

    sigma_rings = [[sigma_ring(h, j) for j in range(chunks)] for h in range(2)]

    def compute(h, j):
        for i in range(chunk):
            s = j * chunk + i
            product = lax.dot_general(
                rg[h][number[s]], w[:, s].reshape(nvec * width, width), (((1,), (1,)), ((), ())),
                preferred_element_type=F32,
            ).reshape(all_terms, part, nvec * width)
            product = jnp.concatenate(
                [product[:, :, v * width:(v + 1) * width] for v in range(nvec)], axis=1
            ).astype(BF16)
            for k in range(all_terms):
                inner[i * rows:(i + 1) * rows, k * width:(k + 1) * width] = product[k]
        total = jnp.dot(
            inner[...], lg[...].reshape(all_terms * width, width), preferred_element_type=F32
        ).astype(BF16)
        sg[h, j, plane] = total
        for i in range(chunk):
            s = j * chunk + i
            turned[h * rows:(h + 1) * rows, s * width:(s + 1) * width] = total[i * rows:(i + 1) * rows]
        sigma_rings[h][j].start()

    def sigma_step(h, d):
        for j in range(chunks):
            sigma_rings[h][j].step(d)

    def assemble(j):
        for i in range(chunk):
            halves = [
                sg[h, j, :, i * rows:(i + 1) * rows].astype(F32).reshape(planes, nvec, part, width) for h in range(2)
            ]
            for v in range(nvec):
                joined = jnp.concatenate([half[:, v].reshape(planes * part, width) for half in halves], axis=0)
                out[v, j * chunk + i] = joined.astype(BF16).T

    stages = [(plane, planes, above), (first, side, along), (second, side, across), (core, 2, [sibling])]

    def reduce_sends(stage):
        mine, n, devices = stages[stage]
        for d in range(1, n):
            send(
                red.at[stage, mine], red.at[stage, mine], red_send.at[stage, d], red_recv.at[stage, d], devices[d - 1]
            )

    def subspace_start():
        row = lax.broadcasted_iota(jnp.int32, (2 * rows, width), 0)
        column = lax.broadcasted_iota(jnp.int32, (2 * rows, width), 1)
        own = column == (row // rows * planes + plane) * part + lax.rem(row, part)
        vector = lax.rem(row, rows) // part
        tile_row = lax.broadcasted_iota(jnp.int32, red.shape[-2:], 0)
        tile_column = lax.broadcasted_iota(jnp.int32, red.shape[-2:], 1)
        tile = jnp.zeros(red.shape[-2:], F32)
        for i in range(nvec):
            product = jnp.dot(
                turned[...], w[i].reshape(sectors * width, width), preferred_element_type=F32
            )
            for j in range(nvec):
                value = jnp.sum(jnp.where(own & (vector == j), product, 0.0), axis=(0, 1), keepdims=True)
                tile = tile + jnp.where((tile_row == i) & (tile_column == j), value, 0.0)
        red[0, plane] = tile
        reduce_sends(0)

    def subspace_stage(stage):
        mine, n, _ = stages[stage]
        for d in range(1, n):
            arrived(red.at[stage, shift(mine, -d, n)], red_send.at[stage, d], red_recv.at[stage, d])
        total = red[stage, 0]
        for i in range(1, n):
            total = total + red[stage, i]
        if stage + 1 < len(stages):
            red[stage + 1, stages[stage + 1][0]] = total
            reduce_sends(stage + 1)
        else:
            sub[...] = total * (1.0 / math.sqrt(2 * side * side * sectors * width * width))

    for j in range(chunks):
        compute(0, j)
    second_arrivals(1)
    sigma_step(0, 1)
    handed(1)
    for j in range(chunks):
        compute(1, j)
    sigma_step(0, 2)
    subspace_start()
    sigma_step(1, 1)
    sigma_step(0, 3)
    subspace_stage(0)
    sigma_step(1, 2)
    sigma_step(0, 4)
    subspace_stage(1)
    sigma_step(1, 3)
    subspace_stage(2)
    for j in range(chunks):
        sigma_rings[1][j].step(4)
        assemble(j)
        if j == 0:
            subspace_stage(3)

    for copy in sends:
        copy.wait_send()
    for each in left + sigma_rings[0] + sigma_rings[1]:
        each.finish()


def body(wavefunction, right_number, left_dim, right_dim, left_ops, right_ops, set_kind, *, chunk=8):
    nvec, sectors, width, _ = wavefunction.shape
    planes = lax.axis_size("ops")
    places = lax.axis_size("sec")
    side = math.isqrt(places // 2)
    terms = left_ops.shape[0]
    part = width // planes // 2
    rows = nvec * part
    chunks = sectors // chunk
    vmem = pl.BlockSpec(memory_space=pltpu.VMEM)
    hbm = pl.BlockSpec(memory_space=pltpu.HBM)
    dma = pltpu.SemaphoreType.DMA
    out, sub = pl.pallas_call(
        functools.partial(kernel, planes, side, chunk),
        out_shape=(
            jax.ShapeDtypeStruct(wavefunction.shape, BF16),
            jax.ShapeDtypeStruct((8, 128), F32),
        ),
        in_specs=[hbm] * 7,
        out_specs=(vmem, vmem),
        scratch_shapes=[
            pltpu.VMEM(wavefunction.shape, BF16),
            pltpu.SMEM((sectors,), jnp.int32),
            pltpu.SMEM(left_dim.shape, jnp.int32),
            pltpu.SMEM(right_dim.shape, jnp.int32),
            pltpu.VMEM(left_ops.shape, BF16),
            pltpu.VMEM(right_ops.shape, BF16),
            pltpu.SMEM(set_kind.shape, jnp.int32),
            pltpu.VMEM((planes, 2, terms * part, width), BF16),
            pltpu.VMEM((places, planes * terms * part, width), BF16),
            pltpu.VMEM((places, planes * terms * part, width), BF16),
            pltpu.VMEM((planes, terms * width, width), BF16),
            pltpu.VMEM((chunk * rows, planes * terms * width), BF16),
            pltpu.VMEM((2, chunks, planes, chunk * rows, width), BF16),
            pltpu.VMEM((2 * rows, sectors * width), BF16),
            pltpu.VMEM((4, max(planes, side, 2), 8, 128), F32),
            dma((7,)),
            dma((2, planes)),
            dma((2, planes)),
            dma((2, side)),
            dma((2, side)),
            dma((2, side, side)),
            dma((2, side, side)),
            dma((2 + 2 * chunks, planes)),
            dma((2 + 2 * chunks, planes)),
            dma((2, side, side)),
            dma((2, side, side)),
            dma((4, max(planes, side, 2))),
            dma((4, max(planes, side, 2))),
        ],
        compiler_params=pltpu.CompilerParams(
            collective_id=0, has_side_effects=True, vmem_limit_bytes=60 * 1024 * 1024
        ),
        cost_estimate=pl.CostEstimate(
            flops=4 * sectors * nvec * terms * width**3, bytes_accessed=6 * 1024 * 1024, transcendentals=0
        ),
    )(wavefunction, right_number.reshape(sectors), left_dim, right_dim, left_ops, right_ops, set_kind)
    return out, sub[:nvec, :nvec]


def solution(mesh):
    return jax.shard_map(
        body,
        mesh=mesh,
        in_specs=(
            P(None, "sec", None, None),
            P("sec", None),
            P("sec"),
            P("sec"),
            P("ops", "sec", None, None),
            P("ops", "sec", None, None),
            P("ops"),
        ),
        out_specs=(P(None, "sec", None, None), P()),
        check_vma=False,
    )
```

time: 90.7 us -> 69 us (0.76)
  Pallas kernels: 81.9 us -> 62.5 us
  local copies, waits for them, and re-layouts: 6.67 us -> 4.39 us
    pallas_call x1, Pallas kernels: 81.9 us -> 62.5 us  [body(): pl.pallas_call(functools.partial(kernel, planes, side, chunk), out_shape=...]
    unnamed x10 -> x1, local copies, waits for them, and re-layouts: 6.11 us -> 3.16 us
where the time goes in v2:
time: 69 us; the launch traced here: 68.8 us
  Pallas kernels  62.5 us (91%)
  local copies, waits for them, and re-layouts  4.39 us (6%)
  between operations  1.93 us (3%)
    pallas_call x1, Pallas kernels, body(): pl.pallas_call(functools.partial(kernel, planes, side, chunk), out_shape=...  62.5 us
    unnamed x1, local copies, waits for them, and re-layouts  3.16 us

profile of v2, /device:TPU:1, one launch (start us, length us, event | category | flops | bytes accessed | tf_op | source)
XLA Modules:
  0.0 68.8 jit_solution(12338447506717544008)
XLA Ops:
  1.9 62.5 %shard_map.86 = (bf16[2,32,128,128]{3,2,1,0:T(8,128)(2,1)}, f32[8,128]{1,0:T(8,128)}) custom-call(bf16[2,32,128,128]{3,2,1,0:T(8,128)(2,1)} %w_hbm.1, s32[32]{0:T(128)} %bitcast.1, s32[1]{0:T(128)S(6)} %copy.10.left_dim_hbm, s32[1]{0:T(128)S(6)} %copy.11.right_dim_hbm, bf16[4,1,128,128]{3,2,1,0:T(8,128)(2,1)} %left_hbm.1, ...), custom_call_target="tpu_custom_call" | custom-call | flops 2147483648 | bytes 6291456 | tf_op jit(solution)/shard_map/pallas_call | solution.py:367
  64.4 1.2 %slice.3 = f32[2,2]{1,0:T(2,128)} slice(f32[8,128]{1,0:T(8,128)} %get-tuple-element.5), slice={[0:2], [0:2]} | slice | bytes 32 | tf_op jit(solution)/shard_map/slice | solution.py:412
  65.6 3.2 %copy.12 = bf16[2,32,128,128]{3,2,1,0:T(8,128)(2,1)} copy(bf16[2,32,128,128]{3,2,1,0:T(8,128)(2,1)} %get-tuple-element.8) | data formatting | bytes 4194304

commit v3 on v2

v3 whole, which is shorter than its diff:
```python
import functools
import math

import jax
import jax.numpy as jnp
from jax import lax
from jax.experimental import pallas as pl
from jax.experimental.pallas import tpu as pltpu
from jax.sharding import PartitionSpec as P

MESH = pl.DeviceIdType.MESH
BF16 = jnp.bfloat16
F32 = jnp.float32


def remote(src, dst, send, recv, device):
    return pltpu.make_async_remote_copy(
        src_ref=src, dst_ref=dst, send_sem=send, recv_sem=recv, device_id=device, device_id_type=MESH
    )


class Ring:
    def __init__(self, n, me, device, slot, half, send, recv):
        self.n, self.me, self.device = n, me, device
        self.slot, self.half, self.send, self.recv = slot, half, send, recv

    def at(self, offset):
        return lax.rem(self.me + (offset + self.n), self.n)

    def ref(self, offset, distance, way):
        if 2 * distance == self.n:
            return self.half(self.at(offset), way)
        return self.slot(self.at(offset))

    def copy(self, offset, distance, way):
        block = self.ref(offset, distance, way)
        index = way * (self.n // 2) + distance - 1
        return remote(block, block, self.send, self.recv(index), self.device(self.at(1 if way == 0 else -1)))

    def pass_on(self, distance, way):
        step = 1 if way == 0 else -1
        self.copy(-step * (distance - 1), distance, way).start()

    def start(self):
        if self.n > 1:
            self.pass_on(1, 0)
            self.pass_on(1, 1)

    def step(self, distance):
        if 2 * distance > self.n:
            return
        for way in range(2):
            self.copy(-distance if way == 0 else distance, distance, way).wait_recv()
            if 2 * (distance + 1) <= self.n:
                self.pass_on(distance + 1, way)


def kernel(
    planes, side, chunk,
    left_dim, right_dim, w_hbm, number_hbm, kind_hbm, left_hbm, right_hbm,
    out, sub,
    w, number, kind, left_ops, right_ops, rt, rg_low, rg_high, lg, inner, sg, picked, red,
    in_sem, a2a_send, a2a_recv, first_send, first_recv, second_send, second_recv,
    left_send, left_recv, sigma_send, sigma_recv, sib_send, sib_recv, red_send, red_recv,
):
    rg = (rg_low, rg_high)
    terms, width = left_ops.shape[0], left_ops.shape[-1]
    nvec, sectors = w.shape[0], w.shape[1]
    part = width // planes // 2
    rows = nvec * part
    span = terms * part
    chunks = sectors // chunk
    all_terms = terms * planes
    plane = lax.axis_index("ops")
    place = lax.axis_index("sec")
    core = lax.rem(place, 2)
    chip = place // 2
    px, py = lax.rem(chip, side), chip // side
    first = px * (1 - core) + py * core
    second = py * (1 - core) + px * core

    def sector_of(one, two):
        x = one * (1 - core) + two * core
        y = two * (1 - core) + one * core
        return 2 * (y * side + x) + core

    def shift(base, offset, n):
        return lax.rem(base + (offset + n), n)

    above = [{"ops": shift(plane, d, planes)} for d in range(1, planes)]
    along = [{"sec": sector_of(shift(first, d, side), second)} for d in range(1, side)]
    across = [{"sec": sector_of(first, shift(second, d, side))} for d in range(1, side)]
    sibling = {"sec": place + 1 - 2 * core}

    barrier = pltpu.get_barrier_semaphore()
    partners = above + along + across + [sibling]
    for device in partners:
        pl.semaphore_signal(barrier, inc=1, device_id=device, device_id_type=MESH)

    loads = [
        pltpu.make_async_copy(a, b, in_sem.at[i])
        for i, (a, b) in enumerate([
            (right_hbm, right_ops), (kind_hbm, kind), (left_hbm, left_ops), (number_hbm, number), (w_hbm, w)
        ])
    ]
    for copy in loads:
        copy.start()

    lane = lax.broadcasted_iota(jnp.int32, (width, width), 1)
    sub_lane = lax.broadcasted_iota(jnp.int32, (width, width), 0)
    loads[0].wait()
    right_keep = (lane < right_dim[0]) & (sub_lane < right_dim[0])
    blocks = [jnp.where(right_keep, right_ops[k, 0].astype(F32), 0.0).T for k in range(terms)]
    for o in range(planes):
        for h in range(2):
            low = (h * planes + o) * part
            rt[h, o] = jnp.concatenate([block[low:low + part] for block in blocks], axis=0).astype(BF16)

    def at(c, one, two):
        return (c * side + one) * side + two

    mine = at(core, first, second)

    def slot(h, o):
        return rg[h].at[mine, pl.ds(pl.multiple_of(o * span, span), span)]

    for h in range(2):
        rg[h][mine, pl.ds(pl.multiple_of(plane * span, span), span)] = rt[h, plane]
    for copy in loads[1:3]:
        copy.wait()
    left_keep = (lane < left_dim[0]) & (sub_lane < left_dim[0])
    for k in range(terms):
        block = jnp.where(left_keep, left_ops[k, 0].astype(F32), 0.0)
        normal = (jnp.zeros((width, width), jnp.int32) + kind[k]) == 0
        lg[plane, k * width:(k + 1) * width] = jnp.where(normal, block.T, block).astype(BF16)

    pl.semaphore_wait(barrier, len(partners))

    def wait_for(ref, semaphore):
        remote(ref, ref, semaphore, semaphore, sibling).wait_recv()

    far_first = sorted(range(1, planes), key=lambda d: -min(d, planes - d))
    for h in range(2):
        for d in far_first:
            to = shift(plane, d, planes)
            remote(rt.at[h, to], slot(h, plane), a2a_send.at[h], a2a_recv.at[h], {"ops": to}).start()

    pieces = 2
    deep = terms * width // pieces

    def left_ring(i):
        return Ring(
            planes, plane, lambda q: {"ops": q},
            lambda q: lg.at[q, pl.ds(i * deep, deep)],
            lambda q, h: lg.at[q, pl.ds(i * deep + h * (deep // 2), deep // 2)],
            left_send.at[0], lambda index: left_recv.at[i, index],
        )

    left = [left_ring(i) for i in range(pieces)]

    def left_step(d):
        for each in left:
            each.step(d)

    for each in left:
        each.start()

    order = [d for d in (1, 3, 2) if d < side]

    def first_sends(h):
        block = rg[h].at[mine]
        for d in reversed(order):
            remote(block, block, first_send.at[h], first_recv.at[h, d], along[d - 1]).start()

    def second_sends(h, j):
        block = rg[h].at[at(core, shift(first, -j, side), second)]
        for d in order:
            remote(block, block, second_send.at[h], second_recv.at[h, j], across[d - 1]).start()

    def line_arrival(h, j):
        wait_for(rg[h].at[pl.ds(0, side - 1)], second_recv.at[h, j])
        line = rg[h].at[pl.ds(at(core, shift(first, -j, side), 0), side)]
        remote(line, line, sib_send.at[h], sib_recv.at[h], sibling).start()

    for h in range(2):
        wait_for(rt.at[h, pl.ds(0, planes - 1)], a2a_recv.at[h])
        first_sends(h)
        second_sends(h, 0)
    left_step(1)
    for h in range(2):
        for j in order:
            wait_for(rg[h].at[0], first_recv.at[h, j])
            second_sends(h, j)
        if h == 0:
            left_step(2)

    for copy in loads[3:]:
        copy.wait()
    pick_row = lax.broadcasted_iota(jnp.int32, (2 * part, width), 0)
    pick_lane = lax.broadcasted_iota(jnp.int32, (2 * part, width), 1)
    pick = jnp.where(
        pick_lane == (pick_row // part * planes + plane) * part + lax.rem(pick_row, part), 1.0, 0.0
    ).astype(BF16)

    def pick_sectors(low, high):
        for s in range(low, high):
            picked[s] = lax.dot_general(
                pick, w[:, s].reshape(nvec * width, width), (((1,), (1,)), ((), ())), preferred_element_type=F32
            )

    pick_sectors(0, sectors // 2)
    line_arrival(0, 0)
    left_step(3)
    pick_sectors(sectors // 2, sectors)
    for j in order:
        line_arrival(0, j)
    left_step(4)
    half_blocks = side * side
    wait_for(rg[0].at[pl.ds(0, half_blocks)], sib_recv.at[0])

    def sigma_ring(h, j):
        half = chunk * rows // 2
        return Ring(
            planes, plane, lambda q: {"ops": q},
            lambda q: sg.at[h, j, q], lambda q, way: sg.at[h, j, q, pl.ds(way * half, half)],
            sigma_send.at[0], lambda index: sigma_recv.at[h, j, index],
        )

    sigma_rings = [[sigma_ring(h, j) for j in range(chunks)] for h in range(2)]
    traces = [[jnp.zeros((part, width), F32) for _ in range(nvec)] for _ in range(nvec)]

    def right_of(s):
        r = number[s]
        c = lax.rem(r, 2)
        x, y = lax.rem(r // 2, side), r // 2 // side
        return at(c, x * (1 - c) + y * c, y * (1 - c) + x * c)

    def compute(h, j):
        for i in range(chunk):
            s = j * chunk + i
            product = lax.dot_general(
                rg[h][right_of(s)], w[:, s].reshape(nvec * width, width), (((1,), (1,)), ((), ())),
                preferred_element_type=F32,
            ).reshape(all_terms, part, nvec * width)
            product = jnp.concatenate(
                [product[:, :, v * width:(v + 1) * width] for v in range(nvec)], axis=1
            ).astype(BF16)
            for k in range(all_terms):
                inner[i * rows:(i + 1) * rows, k * width:(k + 1) * width] = product[k]
        total = jnp.dot(
            inner[...], lg[...].reshape(all_terms * width, width), preferred_element_type=F32
        ).astype(BF16)
        sg[h, j, plane] = total
        sigma_rings[h][j].start()
        total = total.astype(F32).reshape(chunk, nvec, part, width)
        for i in range(nvec):
            other = picked[j * chunk:(j + 1) * chunk, h * part:(h + 1) * part, i * width:(i + 1) * width]
            for v in range(nvec):
                traces[i][v] = traces[i][v] + jnp.sum(other * total[:, v], axis=0)

    def sigma_step(h, d):
        for j in range(chunks):
            sigma_rings[h][j].step(d)

    def assemble(j):
        for i in range(chunk):
            halves = [
                sg[h, j, :, i * rows:(i + 1) * rows].astype(F32).reshape(planes, nvec, part, width) for h in range(2)
            ]
            for v in range(nvec):
                joined = jnp.concatenate([half[:, v].reshape(planes * part, width) for half in halves], axis=0)
                out[v, j * chunk + i] = joined.astype(BF16).T

    stages = [(plane, planes, above), (first, side, along), (second, side, across), (core, 2, [sibling])]

    def reduce_sends(stage):
        me, n, devices = stages[stage]
        for d in range(1, n):
            remote(
                red.at[stage, me], red.at[stage, me], red_send.at[stage], red_recv.at[stage], devices[d - 1]
            ).start()

    def subspace_start():
        tile_row = lax.broadcasted_iota(jnp.int32, red.shape[-2:], 0)
        tile_column = lax.broadcasted_iota(jnp.int32, red.shape[-2:], 1)
        tile = jnp.zeros(red.shape[-2:], F32)
        for i in range(nvec):
            for v in range(nvec):
                value = jnp.sum(traces[i][v], axis=(0, 1), keepdims=True)
                tile = tile + jnp.where((tile_row == i) & (tile_column == v), value, 0.0)
        red[0, plane] = tile
        reduce_sends(0)

    def subspace_stage(stage):
        _, n, _ = stages[stage]
        wait_for(red.at[stage, pl.ds(0, n - 1)], red_recv.at[stage])
        total = red[stage, 0]
        for i in range(1, n):
            total = total + red[stage, i]
        if stage + 1 < len(stages):
            red[stage + 1, stages[stage + 1][0]] = total
            reduce_sends(stage + 1)
        else:
            sub[...] = total * (1.0 / math.sqrt(2 * side * side * sectors * width * width))

    for j in range(chunks):
        compute(0, j)
    for j in [0] + order:
        line_arrival(1, j)
    sigma_step(0, 1)
    wait_for(rg[1].at[pl.ds(0, half_blocks)], sib_recv.at[1])
    for j in range(chunks):
        compute(1, j)
    subspace_start()
    sigma_step(0, 2)
    sigma_step(1, 1)
    sigma_step(0, 3)
    subspace_stage(0)
    sigma_step(1, 2)
    sigma_step(0, 4)
    subspace_stage(1)
    sigma_step(1, 3)
    subspace_stage(2)

    for h in range(2):
        wait_for(rt.at[h, pl.ds(0, planes - 1)], a2a_send.at[h])
        wait_for(rg[h].at[pl.ds(0, side - 1)], first_send.at[h])
        wait_for(rg[h].at[pl.ds(0, side * (side - 1))], second_send.at[h])
        wait_for(rg[h].at[pl.ds(0, half_blocks)], sib_send.at[h])
    wait_for(lg.at[pl.ds(0, planes - 1)], left_send.at[0])
    for j in range(chunks):
        sigma_rings[1][j].step(4)
        assemble(j)
        if j == 0:
            subspace_stage(3)
    wait_for(sg.at[:, :, pl.ds(0, planes - 1)], sigma_send.at[0])
    for stage, (_, n, _) in enumerate(stages):
        wait_for(red.at[stage, pl.ds(0, n - 1)], red_send.at[stage])


def body(wavefunction, right_number, left_dim, right_dim, left_ops, right_ops, set_kind, *, chunk=16):
    nvec, sectors, width, _ = wavefunction.shape
    planes = lax.axis_size("ops")
    places = lax.axis_size("sec")
    side = math.isqrt(places // 2)
    terms = left_ops.shape[0]
    part = width // planes // 2
    rows = nvec * part
    chunks = sectors // chunk
    vmem = pl.BlockSpec(memory_space=pltpu.VMEM)
    smem = pl.BlockSpec(memory_space=pltpu.SMEM)
    hbm = pl.BlockSpec(memory_space=pltpu.HBM)
    dma = pltpu.SemaphoreType.DMA
    out, sub = pl.pallas_call(
        functools.partial(kernel, planes, side, chunk),
        out_shape=(
            jax.ShapeDtypeStruct(wavefunction.shape, BF16),
            jax.ShapeDtypeStruct((8, 128), F32),
        ),
        in_specs=[smem] * 2 + [hbm] * 5,
        out_specs=(vmem, vmem),
        scratch_shapes=[
            pltpu.VMEM(wavefunction.shape, BF16),
            pltpu.SMEM((sectors,), jnp.int32),
            pltpu.SMEM(set_kind.shape, jnp.int32),
            pltpu.VMEM(left_ops.shape, BF16),
            pltpu.VMEM(right_ops.shape, BF16),
            pltpu.VMEM((2, planes, terms * part, width), BF16),
            pltpu.VMEM((places, planes * terms * part, width), BF16),
            pltpu.VMEM((places, planes * terms * part, width), BF16),
            pltpu.VMEM((planes, terms * width, width), BF16),
            pltpu.VMEM((chunk * rows, planes * terms * width), BF16),
            pltpu.VMEM((2, chunks, planes, chunk * rows, width), BF16),
            pltpu.VMEM((sectors, 2 * part, nvec * width), F32),
            pltpu.VMEM((4, max(planes, side, 2), 8, 128), F32),
            dma((5,)),
            dma((2,)),
            dma((2,)),
            dma((2,)),
            dma((2, side)),
            dma((2,)),
            dma((2, side)),
            dma((1,)),
            dma((2, planes)),
            dma((1,)),
            dma((2, chunks, planes)),
            dma((2,)),
            dma((2,)),
            dma((4,)),
            dma((4,)),
        ],
        compiler_params=pltpu.CompilerParams(
            collective_id=0, has_side_effects=True, vmem_limit_bytes=48 * 1024 * 1024
        ),
        cost_estimate=pl.CostEstimate(
            flops=4 * sectors * nvec * terms * width**3, bytes_accessed=6 * 1024 * 1024, transcendentals=0
        ),
    )(left_dim, right_dim, *[
        pltpu.with_memory_space_constraint(each, pltpu.HBM)
        for each in (
            wavefunction, right_number.reshape(sectors), set_kind, left_ops, right_ops
        )
    ])
    return out, sub[:nvec, :nvec]


def solution(mesh):
    return jax.shard_map(
        body,
        mesh=mesh,
        in_specs=(
            P(None, "sec", None, None),
            P("sec", None),
            P("sec"),
            P("sec"),
            P("ops", "sec", None, None),
            P("ops", "sec", None, None),
            P("ops"),
        ),
        out_specs=(P(None, "sec", None, None), P()),
        check_vma=False,
    )
```

time: 69 us -> 60.1 us (0.87)
  Pallas kernels: 62.5 us -> 56.2 us
  local copies, waits for them, and re-layouts: 4.39 us -> 1.88 us
    pallas_call x1, Pallas kernels: 62.5 us -> 56.2 us  [body(): pl.pallas_call(functools.partial(kernel, planes, side, chunk), out_shape=...]
    unnamed x1, local copies, waits for them, and re-layouts: 3.16 us -> 1.32 us
where the time goes in v3:
time: 60.1 us; the launch traced here: 60 us
  Pallas kernels  56.2 us (94%)
  between operations  1.93 us (3%)
  local copies, waits for them, and re-layouts  1.88 us (3%)
    pallas_call x1, Pallas kernels, body(): pl.pallas_call(functools.partial(kernel, planes, side, chunk), out_shape=...  56.2 us
    unnamed x1, local copies, waits for them, and re-layouts  1.32 us

profile of v3, /device:TPU:1, one launch (start us, length us, event | category | flops | bytes accessed | tf_op | source)
XLA Modules:
  0.0 60.0 jit_solution(2310560317450648446)
XLA Ops:
  1.9 56.2 %shard_map.86 = (bf16[2,32,128,128]{3,2,1,0:T(8,128)(2,1)S(1)}, f32[8,128]{1,0:T(8,128)S(1)}) custom-call(s32[1]{0:T(128)S(6)} %copy.10.left_dim, s32[1]{0:T(128)S(6)} %copy.11.right_dim, bf16[2,32,128,128]{3,2,1,0:T(8,128)(2,1)} %w_hbm.1, s32[32]{0:T(128)} %bitcast.1, s32[4]{0:T(128)} %kind_hbm.1, bf16[4,1,128,128]{3,2,1,0:T(8,128)(2,1)} %left_hbm.1, ...), custom_call_target="tpu_custom_call" | custom-call | flops 2147483648 | bytes 6291456 | tf_op jit(solution)/shard_map/pallas_call | solution.py:354
  58.1 0.6 slice.3
  58.7 1.3 %copy.12 = bf16[2,32,128,128]{3,2,1,0:T(8,128)(2,1)} copy(bf16[2,32,128,128]{3,2,1,0:T(8,128)(2,1)S(1)} %get-tuple-element.8) | data formatting | bytes 4194304

commit v4 on v3

--- a/solution.py
+++ b/solution.py
@@ -126,6 +126,19 @@
 
     for h in range(2):
         rg[h][mine, pl.ds(pl.multiple_of(plane * span, span), span)] = rt[h, plane]
+
+    pl.semaphore_wait(barrier, len(partners))
+
+    def wait_for(ref, semaphore):
+        remote(ref, ref, semaphore, semaphore, sibling).wait_recv()
+
+    far_first = sorted(range(1, planes), key=lambda d: -min(d, planes - d))
+    def slices(h):
+        for d in far_first:
+            to = shift(plane, d, planes)
+            remote(rt.at[h, to], slot(h, plane), a2a_send.at[h], a2a_recv.at[h], {"ops": to}).start()
+
+    slices(0)
     for copy in loads[1:3]:
         copy.wait()
     left_keep = (lane < left_dim[0]) & (sub_lane < left_dim[0])
@@ -134,16 +147,7 @@
         normal = (jnp.zeros((width, width), jnp.int32) + kind[k]) == 0
         lg[plane, k * width:(k + 1) * width] = jnp.where(normal, block.T, block).astype(BF16)
 
-    pl.semaphore_wait(barrier, len(partners))
-
-    def wait_for(ref, semaphore):
-        remote(ref, ref, semaphore, semaphore, sibling).wait_recv()
-
-    far_first = sorted(range(1, planes), key=lambda d: -min(d, planes - d))
-    for h in range(2):
-        for d in far_first:
-            to = shift(plane, d, planes)
-            remote(rt.at[h, to], slot(h, plane), a2a_send.at[h], a2a_recv.at[h], {"ops": to}).start()
+    slices(1)
 
     pieces = 2
     deep = terms * width // pieces
@@ -182,18 +186,6 @@
         line = rg[h].at[pl.ds(at(core, shift(first, -j, side), 0), side)]
         remote(line, line, sib_send.at[h], sib_recv.at[h], sibling).start()
 
-    for h in range(2):
-        wait_for(rt.at[h, pl.ds(0, planes - 1)], a2a_recv.at[h])
-        first_sends(h)
-        second_sends(h, 0)
-    left_step(1)
-    for h in range(2):
-        for j in order:
-            wait_for(rg[h].at[0], first_recv.at[h, j])
-            second_sends(h, j)
-        if h == 0:
-            left_step(2)
-
     for copy in loads[3:]:
         copy.wait()
     pick_row = lax.broadcasted_iota(jnp.int32, (2 * part, width), 0)
@@ -208,10 +200,26 @@
                 pick, w[:, s].reshape(nvec * width, width), (((1,), (1,)), ((), ())), preferred_element_type=F32
             )
 
-    pick_sectors(0, sectors // 2)
+    def first_arrivals(h):
+        for j in order:
+            wait_for(rg[h].at[0], first_recv.at[h, j])
+            second_sends(h, j)
+
+    pick_sectors(0, 8)
+    wait_for(rt.at[0, pl.ds(0, planes - 1)], a2a_recv.at[0])
+    first_sends(0)
+    pick_sectors(8, 16)
+    second_sends(0, 0)
+    wait_for(rt.at[1, pl.ds(0, planes - 1)], a2a_recv.at[1])
+    first_sends(1)
+    left_step(1)
+    first_arrivals(0)
+    second_sends(1, 0)
+    left_step(2)
+    first_arrivals(1)
     line_arrival(0, 0)
     left_step(3)
-    pick_sectors(sectors // 2, sectors)
+    pick_sectors(16, sectors)
     for j in order:
         line_arrival(0, j)
     left_step(4)
@@ -252,7 +260,9 @@
         ).astype(BF16)
         sg[h, j, plane] = total
         sigma_rings[h][j].start()
-        total = total.astype(F32).reshape(chunk, nvec, part, width)
+
+    def trace(h, j):
+        total = sg[h, j, plane].astype(F32).reshape(chunk, nvec, part, width)
         for i in range(nvec):
             other = picked[j * chunk:(j + 1) * chunk, h * part:(h + 1) * part, i * width:(i + 1) * width]
             for v in range(nvec):
@@ -305,12 +315,16 @@
 
     for j in range(chunks):
         compute(0, j)
+    for j in range(chunks):
+        trace(0, j)
     for j in [0] + order:
         line_arrival(1, j)
     sigma_step(0, 1)
     wait_for(rg[1].at[pl.ds(0, half_blocks)], sib_recv.at[1])
     for j in range(chunks):
         compute(1, j)
+    for j in range(chunks):
+        trace(1, j)
     subspace_start()
     sigma_step(0, 2)
     sigma_step(1, 1)

time: 60.1 us -> 59.8 us (level)
  no operation moved by 1% of the time
where the time goes in v4:
time: 59.8 us; the launch traced here: 59.7 us
  Pallas kernels  55.9 us (93%)
  between operations  1.93 us (3%)
  local copies, waits for them, and re-layouts  1.88 us (3%)
    pallas_call x1, Pallas kernels, body(): pl.pallas_call(functools.partial(kernel, planes, side, chunk), out_shape=...  55.9 us
    unnamed x1, local copies, waits for them, and re-layouts  1.32 us

profile of v4, /device:TPU:1, one launch (start us, length us, event | category | flops | bytes accessed | tf_op | source)
XLA Modules:
  0.0 59.7 jit_solution(2123055083101274656)
XLA Ops:
  1.9 55.9 %shard_map.86 = (bf16[2,32,128,128]{3,2,1,0:T(8,128)(2,1)S(1)}, f32[8,128]{1,0:T(8,128)S(1)}) custom-call(s32[1]{0:T(128)S(6)} %copy.10.left_dim, s32[1]{0:T(128)S(6)} %copy.11.right_dim, bf16[2,32,128,128]{3,2,1,0:T(8,128)(2,1)} %w_hbm.1, s32[32]{0:T(128)} %bitcast.1, s32[4]{0:T(128)} %kind_hbm.1, bf16[4,1,128,128]{3,2,1,0:T(8,128)(2,1)} %left_hbm.1, ...), custom_call_target="tpu_custom_call" | custom-call | flops 2147483648 | bytes 6291456 | tf_op jit(solution)/shard_map/pallas_call | solution.py:368
  57.8 0.6 slice.3
  58.4 1.3 %copy.12 = bf16[2,32,128,128]{3,2,1,0:T(8,128)(2,1)} copy(bf16[2,32,128,128]{3,2,1,0:T(8,128)(2,1)S(1)} %get-tuple-element.8) | data formatting | bytes 4194304

commit v5 on v4

--- a/solution.py
+++ b/solution.py
@@ -147,7 +147,6 @@
         normal = (jnp.zeros((width, width), jnp.int32) + kind[k]) == 0
         lg[plane, k * width:(k + 1) * width] = jnp.where(normal, block.T, block).astype(BF16)
 
-    slices(1)
 
     pieces = 2
     deep = terms * width // pieces
@@ -166,8 +165,6 @@
         for each in left:
             each.step(d)
 
-    for each in left:
-        each.start()
 
     order = [d for d in (1, 3, 2) if d < side]
 
@@ -206,6 +203,9 @@
             second_sends(h, j)
 
     pick_sectors(0, 8)
+    slices(1)
+    for each in left:
+        each.start()
     wait_for(rt.at[0, pl.ds(0, planes - 1)], a2a_recv.at[0])
     first_sends(0)
     pick_sectors(8, 16)

time: 59.8 us -> 59.8 us (level)
  no operation moved by 1% of the time
where the time goes in v5:
time: 59.8 us; the launch traced here: 59.6 us
  Pallas kernels  55.8 us (93%)
  between operations  1.93 us (3%)
  local copies, waits for them, and re-layouts  1.88 us (3%)
    pallas_call x1, Pallas kernels, body(): pl.pallas_call(functools.partial(kernel, planes, side, chunk), out_shape=...  55.8 us
    unnamed x1, local copies, waits for them, and re-layouts  1.32 us

profile of v5, /device:TPU:1, one launch (start us, length us, event | category | flops | bytes accessed | tf_op | source)
XLA Modules:
  0.0 59.6 jit_solution(7351427328333055360)
XLA Ops:
  1.9 55.8 %shard_map.86 = (bf16[2,32,128,128]{3,2,1,0:T(8,128)(2,1)S(1)}, f32[8,128]{1,0:T(8,128)S(1)}) custom-call(s32[1]{0:T(128)S(6)} %copy.10.left_dim, s32[1]{0:T(128)S(6)} %copy.11.right_dim, bf16[2,32,128,128]{3,2,1,0:T(8,128)(2,1)} %w_hbm.1, s32[32]{0:T(128)} %bitcast.1, s32[4]{0:T(128)} %kind_hbm.1, bf16[4,1,128,128]{3,2,1,0:T(8,128)(2,1)} %left_hbm.1, ...), custom_call_target="tpu_custom_call" | custom-call | flops 2147483648 | bytes 6291456 | tf_op jit(solution)/shard_map/pallas_call | solution.py:368
  57.7 0.6 slice.3
  58.3 1.3 %copy.12 = bf16[2,32,128,128]{3,2,1,0:T(8,128)(2,1)} copy(bf16[2,32,128,128]{3,2,1,0:T(8,128)(2,1)S(1)} %get-tuple-element.8) | data formatting | bytes 4194304
